TPU v7x, 32 devices: a whole 2x2x4 slice. The times are simulated.
32 devices in a mesh: ctx: 8 (over y, x, core), ch: 4 (over z).
Axes of the slice: x: 2, y: 2, z: 4, core: 2. Of those that a mesh axis runs over, the one named last changes fastest.
Arguments:
- q_proj: bfloat16 [4096, 4096], P(('ctx', 'ch')), may hold values from -6 to 6
- k_proj: bfloat16 [4096, 4096], P(('ctx', 'ch')), may hold values from -6 to 6
- v_proj: bfloat16 [4096, 4096], P(('ctx', 'ch')), may hold values from -6 to 6
- filter_taps: bfloat16 [4096, 4096], P(('ctx', 'ch')), may hold values from -6 to 6
- out_grad: bfloat16 [4096, 4096], P(('ctx', 'ch')), may hold values from -6 to 6
Outputs:
- mixed: bfloat16 [4096, 4096], P(('ctx', 'ch'))
- q_grad: bfloat16 [4096, 4096], P(('ctx', 'ch'))
- k_grad: bfloat16 [4096, 4096], P(('ctx', 'ch'))
- v_grad: bfloat16 [4096, 4096], P(('ctx', 'ch'))
- filter_grad: bfloat16 [4096, 4096], P(('ctx', 'ch'))
All inputs are finite; a program needn't handle non-finite values.
Results may differ from a plain program's by a relative error of at most 0.013.
Values may be sent and summed in bfloat16 or wider, within the bound.
A program may use at most 192 MiB of HBM per device.

v0:
```python
import functools
import math

import jax
import jax.numpy as jnp
import numpy as np
from jax import lax
from jax.experimental import pallas as pl
from jax.experimental.pallas import tpu as pltpu
from jax.sharding import PartitionSpec as P

PRECISE = lax.Precision.HIGHEST


def build_tables(first, second):
    points = first * second
    half = first // 2
    rows_first = jnp.arange(first, dtype=jnp.int32)
    rows_half = jnp.arange(half, dtype=jnp.int32)
    rows_second = jnp.arange(second, dtype=jnp.int32)
    outer_phase = rows_first[:, None] * rows_half[None, :] % first
    outer_angle = outer_phase.astype(jnp.float32) * (2.0 * math.pi / first)
    turn_phase = rows_first[:, None] * rows_second[None, :] % points
    turn_angle = turn_phase.astype(jnp.float32) * (2.0 * math.pi / points)
    inner_phase = rows_second[:, None] * rows_second[None, :] % second
    inner_angle = inner_phase.astype(jnp.float32) * (2.0 * math.pi / second)
    return (
        jnp.cos(outer_angle),
        jnp.sin(outer_angle),
        jnp.cos(turn_angle),
        jnp.sin(turn_angle),
        jnp.cos(inner_angle),
        jnp.sin(inner_angle),
    )


def split_table(table):
    upper = table.astype(jnp.bfloat16)
    lower = (table - upper.astype(jnp.float32)).astype(jnp.bfloat16)
    return (upper, lower)


def table_product(table, shaped):
    upper, lower = split_table(table)
    total = jnp.einsum("kn,cnm->ckm", upper, shaped, preferred_element_type=jnp.float32)
    return total + jnp.einsum("kn,cnm->ckm", lower, shaped, preferred_element_type=jnp.float32)


def forward_spectrum(tables, signal):
    outer_cos, outer_sin, turn_cos, turn_sin, inner_cos, inner_sin = tables
    half = outer_cos.shape[1]
    second = inner_cos.shape[0]
    shaped = signal.reshape(signal.shape[0], half, second)
    real_outer = table_product(outer_cos, shaped)
    imag_outer = -table_product(outer_sin, shaped)
    real_turned = real_outer * turn_cos + imag_outer * turn_sin
    imag_turned = imag_outer * turn_cos - real_outer * turn_sin
    real_spec = jnp.einsum(
        "ckn,mn->ckm", real_turned, inner_cos, precision=PRECISE, preferred_element_type=jnp.float32
    )
    real_spec = real_spec + jnp.einsum(
        "ckn,mn->ckm", imag_turned, inner_sin, precision=PRECISE, preferred_element_type=jnp.float32
    )
    imag_spec = jnp.einsum(
        "ckn,mn->ckm", imag_turned, inner_cos, precision=PRECISE, preferred_element_type=jnp.float32
    )
    imag_spec = imag_spec - jnp.einsum(
        "ckn,mn->ckm", real_turned, inner_sin, precision=PRECISE, preferred_element_type=jnp.float32
    )
    return (real_spec, imag_spec)


def inverse_signal(tables, spec_pair):
    outer_cos, outer_sin, turn_cos, turn_sin, inner_cos, inner_sin = tables
    real_spec, imag_spec = spec_pair
    points = outer_cos.shape[0] * inner_cos.shape[0]
    real_inner = jnp.einsum(
        "ckn,mn->ckm", real_spec, inner_cos, precision=PRECISE, preferred_element_type=jnp.float32
    )
    real_inner = real_inner - jnp.einsum(
        "ckn,mn->ckm", imag_spec, inner_sin, precision=PRECISE, preferred_element_type=jnp.float32
    )
    imag_inner = jnp.einsum(
        "ckn,mn->ckm", imag_spec, inner_cos, precision=PRECISE, preferred_element_type=jnp.float32
    )
    imag_inner = imag_inner + jnp.einsum(
        "ckn,mn->ckm", real_spec, inner_sin, precision=PRECISE, preferred_element_type=jnp.float32
    )
    real_turned = real_inner * turn_cos - imag_inner * turn_sin
    imag_turned = imag_inner * turn_cos + real_inner * turn_sin
    result = jnp.einsum(
        "kn,ckm->cnm", outer_cos, real_turned, precision=PRECISE, preferred_element_type=jnp.float32
    )
    result = result - jnp.einsum(
        "kn,ckm->cnm", outer_sin, imag_turned, precision=PRECISE, preferred_element_type=jnp.float32
    )
    return result.reshape(result.shape[0], -1) / points


def product(left_pair, right_pair):
    return (
        left_pair[0] * right_pair[0] - left_pair[1] * right_pair[1],
        left_pair[0] * right_pair[1] + left_pair[1] * right_pair[0],
    )


def product_conj(left_pair, right_pair):
    return (
        left_pair[0] * right_pair[0] + left_pair[1] * right_pair[1],
        left_pair[1] * right_pair[0] - left_pair[0] * right_pair[1],
    )


def forward_inputs(key_rows, value_rows, taps_rows):
    return (
        lax.all_to_all(key_rows, ("ctx", "ch"), split_axis=0, concat_axis=1, tiled=True),
        lax.all_to_all(value_rows, ("ctx", "ch"), split_axis=0, concat_axis=1, tiled=True),
        lax.all_to_all(taps_rows, ("ctx", "ch"), split_axis=0, concat_axis=1, tiled=True),
    )


def backward_inputs(query_rows, grad_rows):
    return (
        lax.all_to_all(query_rows, ("ctx", "ch"), split_axis=0, concat_axis=1, tiled=True),
        lax.all_to_all(grad_rows, ("ctx", "ch"), split_axis=0, concat_axis=1, tiled=True),
    )


def first_outputs(mixed, q_grad):
    moved = (
        lax.all_to_all(mixed, ("ctx", "ch"), split_axis=1, concat_axis=0, tiled=True),
        lax.all_to_all(q_grad, ("ctx", "ch"), split_axis=1, concat_axis=0, tiled=True),
    )
    return tuple((piece.T for piece in moved))


def second_outputs(k_grad, v_grad, filter_grad):
    moved = (
        lax.all_to_all(k_grad, ("ctx", "ch"), split_axis=1, concat_axis=0, tiled=True),
        lax.all_to_all(v_grad, ("ctx", "ch"), split_axis=1, concat_axis=0, tiled=True),
        lax.all_to_all(filter_grad, ("ctx", "ch"), split_axis=1, concat_axis=0, tiled=True),
    )
    return tuple((piece.T for piece in moved))


def general_body(q_proj, k_proj, v_proj, filter_taps, out_grad):
    key_part, value_part, taps_part = forward_inputs(k_proj.T, v_proj.T, filter_taps.T)
    length = key_part.shape[1]
    points = 2 * length
    second = math.gcd(points, 128)
    first = points // second
    tables = build_tables(first, second)
    norm_scale = 1.0 / math.sqrt(length)
    key_wide = key_part.astype(jnp.float32)
    value_wide = value_part.astype(jnp.float32)
    gated = (key_wide * value_wide).astype(jnp.bfloat16)
    gated_spec = forward_spectrum(tables, gated)
    taps_spec = forward_spectrum(tables, taps_part)
    query_part, cotangent = backward_inputs(q_proj.T, out_grad.T)
    query_wide = query_part.astype(jnp.float32)
    grad_wide = cotangent.astype(jnp.float32)
    conv_out = inverse_signal(tables, product(taps_spec, gated_spec)) * norm_scale
    mixed = (query_wide * conv_out).astype(jnp.bfloat16)
    q_grad = (grad_wide * conv_out).astype(jnp.bfloat16)
    mixed, q_grad = first_outputs(mixed, q_grad)
    back_in = (grad_wide * query_wide).astype(jnp.bfloat16)
    back_spec = forward_spectrum(tables, back_in)
    conv_grad = inverse_signal(tables, product_conj(back_spec, taps_spec)) * norm_scale
    filter_grad = (inverse_signal(tables, product_conj(back_spec, gated_spec)) * norm_scale).astype(
        jnp.bfloat16
    )
    k_grad = (conv_grad * value_wide).astype(jnp.bfloat16)
    v_grad = (conv_grad * key_wide).astype(jnp.bfloat16)
    k_grad, v_grad, filter_grad = second_outputs(k_grad, v_grad, filter_grad)
    return (mixed, q_grad, k_grad, v_grad, filter_grad)


MESH_ID = pl.DeviceIdType.MESH
GROUP = 16
BF16 = jnp.bfloat16


def dft_tables(blocks, rows, norm_scale):
    first = 2 * blocks
    points = first * rows
    half = rows // 2
    n1 = np.arange(first)
    outer = np.zeros((first, first))
    outer[0] = 1.0
    outer[1] = np.cos(np.pi * n1)
    for k in range(1, blocks):
        angle = 2.0 * np.pi * (n1 * k % first) / first
        outer[2 * k] = np.cos(angle)
        outer[2 * k + 1] = -np.sin(angle)
    outer_inv = np.linalg.inv(outer)[:blocks] * norm_scale
    outer = outer[:, :blocks]
    n2 = np.arange(rows)
    inner = np.zeros((blocks, 2 * rows, 2 * rows))
    for k in range(1, blocks):
        freq = k + first * np.arange(rows)
        angle = 2.0 * np.pi * (freq[:, None] * n2[None, :] % points) / points
        cos, sin = np.cos(angle), np.sin(angle)
        inner[k] = np.block([[cos, sin], [-sin, cos]])
    for part, k in enumerate((0, blocks)):
        freq = k + first * np.arange(half)
        angle = 2.0 * np.pi * (freq[:, None] * n2[None, :] % points) / points
        columns = slice(part * rows, (part + 1) * rows)
        inner[0, part * half : (part + 1) * half, columns] = np.cos(angle)
        inner[0, rows + part * half : rows + (part + 1) * half, columns] = -np.sin(angle)
    inner[0, rows, :rows] = np.cos(np.pi * n2)
    inner_inv = np.linalg.inv(inner)
    eye = np.eye(GROUP)
    return tuple(
        np.asarray(table, np.float32).astype(BF16)
        for table in (np.kron(outer, eye), inner, inner_inv, np.kron(outer_inv, eye))
    )


def conv_kernel(
    blocks,
    inner_size,
    taps_ref,
    gated_ref,
    back_ref,
    outer_hbm,
    inner_hbm,
    inner_inv_hbm,
    outer_inv_hbm,
    conv_ref,
    cgrad_ref,
    fgrad_ref,
    rx,
    tx,
    mid,
    prod,
    taps_spec,
    gated_spec,
    outer_t,
    inner_t,
    inner_inv_t,
    outer_inv_t,
    table_sem,
    send_sem,
    recv_sem,
):
    rows = taps_ref.shape[0]
    lanes = rx.shape[-1]
    me = lax.axis_index("ctx") * inner_size + lax.axis_index("ch")
    sources = (taps_ref, gated_ref, back_ref)
    results = (conv_ref, cgrad_ref, fgrad_ref)
    tables = (
        (outer_hbm, outer_t),
        (inner_hbm, inner_t),
        (inner_inv_hbm, inner_inv_t),
        (outer_inv_hbm, outer_inv_t),
    )

    def peer_at(step):
        peer = lax.rem(me + step, blocks)
        return peer, (peer // inner_size, lax.rem(peer, inner_size))

    def row_block(index):
        return pl.ds(pl.multiple_of(index * rows, rows), rows)

    def lane_block(index):
        return pl.ds(pl.multiple_of(index * lanes, lanes), lanes)

    def send_in(which):
        pltpu.make_async_copy(
            sources[which].at[:, lane_block(me)], rx.at[which, row_block(me)], recv_sem.at[which]
        ).start()

        @pl.loop(1, blocks)
        def _(step):
            peer, where = peer_at(step)
            pltpu.make_async_remote_copy(
                src_ref=sources[which].at[:, lane_block(peer)],
                dst_ref=rx.at[which, row_block(me)],
                send_sem=send_sem.at[which],
                recv_sem=recv_sem.at[which],
                device_id=where,
                device_id_type=MESH_ID,
            ).start()

    def send_out(which):
        slot = 3 + which
        pltpu.make_async_copy(
            tx.at[which, row_block(me)], results[which].at[:, lane_block(me)], recv_sem.at[slot]
        ).start()

        @pl.loop(1, blocks)
        def _(step):
            peer, where = peer_at(step)
            pltpu.make_async_remote_copy(
                src_ref=tx.at[which, row_block(peer)],
                dst_ref=results[which].at[:, lane_block(me)],
                send_sem=send_sem.at[slot],
                recv_sem=recv_sem.at[slot],
                device_id=where,
                device_id_type=MESH_ID,
            ).start()

    def wait_in(which):
        pltpu.make_async_copy(rx.at[which], rx.at[which], recv_sem.at[which]).wait()

    def wait_out(which):
        pltpu.make_async_copy(results[which], results[which], recv_sem.at[3 + which]).wait()

    def wait_sent(slot):
        part = rx.at[0, pl.ds(0, (blocks - 1) * rows)]
        pltpu.make_async_copy(part, part, send_sem.at[slot]).wait()

    for index, (source, target) in enumerate(tables):
        pltpu.make_async_copy(source, target, table_sem.at[index]).start()

    barrier = pltpu.get_barrier_semaphore()

    @pl.loop(1, blocks)
    def _(step):
        _, where = peer_at(step)
        pl.semaphore_signal(barrier, inc=1, device_id=where, device_id_type=MESH_ID)

    pl.semaphore_wait(barrier, blocks - 1)

    for which in range(3):
        send_in(which)

    for index, (source, target) in enumerate(tables):
        pltpu.make_async_copy(source, target, table_sem.at[index]).wait()

    pairs = rows // (2 * GROUP)

    def outer_stage(which):
        signal = rx.at[which].reshape(blocks, rows, lanes)

        @pl.loop(0, pairs)
        def _(pair):
            low = pl.ds(pl.multiple_of(pair * 2 * GROUP, GROUP), GROUP)
            high = pl.ds(pl.multiple_of(pair * 2 * GROUP + GROUP, GROUP), GROUP)
            data = jnp.concatenate(
                [
                    signal[:, low, :].reshape(blocks * GROUP, lanes),
                    signal[:, high, :].reshape(blocks * GROUP, lanes),
                ],
                axis=1,
            )
            out = jnp.dot(outer_t[...], data, preferred_element_type=jnp.float32).astype(BF16)
            mid[:, low, :] = out[:, :lanes].reshape(2 * blocks, GROUP, lanes)
            mid[:, high, :] = out[:, lanes:].reshape(2 * blocks, GROUP, lanes)

    def spectrum(k):
        data = mid[pl.ds(2 * k, 2)].reshape(2 * rows, lanes)
        return jnp.dot(inner_t[k], data, preferred_element_type=jnp.float32)

    def real_row(k):
        row = lax.broadcasted_iota(jnp.int32, (rows, lanes), 0)
        return jnp.logical_and(row == 0, k == 0)

    def multiply(left, right, alone):
        lr, li = left[:rows], left[rows:]
        rr, ri = right[:rows], right[rows:]
        real, cross = lr * rr, li * ri
        return jnp.concatenate(
            [jnp.where(alone, real, real - cross), jnp.where(alone, cross, lr * ri + li * rr)], axis=0
        ).astype(BF16)

    def multiply_conj(left, right, alone):
        lr, li = left[:rows], left[rows:]
        rr, ri = right[:rows], right[rows:]
        real, cross = lr * rr, li * ri
        return jnp.concatenate(
            [jnp.where(alone, real, real + cross), jnp.where(alone, cross, li * rr - lr * ri)], axis=0
        ).astype(BF16)

    def inverse_outer(which, slot):
        signal = tx.at[which].reshape(blocks, rows, lanes)

        @pl.loop(0, pairs)
        def _(pair):
            low = pl.ds(pl.multiple_of(pair * 2 * GROUP, GROUP), GROUP)
            high = pl.ds(pl.multiple_of(pair * 2 * GROUP + GROUP, GROUP), GROUP)
            data = jnp.concatenate(
                [
                    prod[slot, :, low, :].reshape(2 * blocks * GROUP, lanes),
                    prod[slot, :, high, :].reshape(2 * blocks * GROUP, lanes),
                ],
                axis=1,
            )
            out = jnp.dot(outer_inv_t[...], data, preferred_element_type=jnp.float32).astype(BF16)
            signal[:, low, :] = out[:, :lanes].reshape(blocks, GROUP, lanes)
            signal[:, high, :] = out[:, lanes:].reshape(blocks, GROUP, lanes)

    wait_in(0)
    outer_stage(0)

    @pl.loop(0, blocks)
    def _(k):
        taps_spec[k] = spectrum(k)

    wait_in(1)
    outer_stage(1)

    @pl.loop(0, blocks)
    def _(k):
        spec = spectrum(k)
        gated_spec[k] = spec
        pair = multiply(taps_spec[k], spec, real_row(k))
        out = jnp.dot(inner_inv_t[k], pair, preferred_element_type=jnp.float32)
        prod[0, pl.ds(2 * k, 2)] = out.astype(BF16).reshape(2, rows, lanes)

    inverse_outer(0, 0)
    send_out(0)

    wait_in(2)
    outer_stage(2)

    @pl.loop(0, blocks)
    def _(k):
        spec = spectrum(k)
        alone = real_row(k)
        pair = jnp.concatenate(
            [multiply_conj(spec, taps_spec[k], alone), multiply_conj(spec, gated_spec[k], alone)], axis=1
        )
        out = jnp.dot(inner_inv_t[k], pair, preferred_element_type=jnp.float32).astype(BF16)
        prod[0, pl.ds(2 * k, 2)] = out[:, :lanes].reshape(2, rows, lanes)
        prod[1, pl.ds(2 * k, 2)] = out[:, lanes:].reshape(2, rows, lanes)

    inverse_outer(1, 0)
    send_out(1)
    inverse_outer(2, 1)
    send_out(2)

    for slot in range(6):
        wait_sent(slot)
    for which in range(3):
        wait_out(which)


def convolve(taps, gated, back_in, blocks, inner_size):
    rows, channels = taps.shape
    lanes = channels // blocks
    norm_scale = 1.0 / math.sqrt(rows * blocks)
    tables = dft_tables(blocks, rows, norm_scale)
    signal = jax.ShapeDtypeStruct((rows, channels), BF16)
    anywhere = pl.BlockSpec(memory_space=pl.ANY)
    flops = 2 * lanes * 2 * rows * blocks * (9 * 2 * rows + 6 * blocks * GROUP)
    return pl.pallas_call(
        functools.partial(conv_kernel, blocks, inner_size),
        out_shape=(signal, signal, signal),
        in_specs=[anywhere] * 7,
        out_specs=(anywhere, anywhere, anywhere),
        scratch_shapes=[
            pltpu.VMEM((3, blocks * rows, lanes), BF16),
            pltpu.VMEM((3, blocks * rows, lanes), BF16),
            pltpu.VMEM((2 * blocks, rows, lanes), BF16),
            pltpu.VMEM((2, 2 * blocks, rows, lanes), BF16),
            pltpu.VMEM((blocks, 2 * rows, lanes), jnp.float32),
            pltpu.VMEM((blocks, 2 * rows, lanes), jnp.float32),
        ]
        + [pltpu.VMEM(table.shape, BF16) for table in tables]
        + [
            pltpu.SemaphoreType.DMA((4,)),
            pltpu.SemaphoreType.DMA((6,)),
            pltpu.SemaphoreType.DMA((6,)),
        ],
        compiler_params=pltpu.CompilerParams(
            collective_id=0, has_side_effects=True, vmem_limit_bytes=48 * 1024 * 1024
        ),
        cost_estimate=pl.CostEstimate(flops=flops, bytes_accessed=32 * rows * channels, transcendentals=0),
    )(taps, gated, back_in, *(jnp.asarray(table) for table in tables))


def fast_body(blocks, inner_size, q_proj, k_proj, v_proj, filter_taps, out_grad):
    query = q_proj.astype(jnp.float32)
    key = k_proj.astype(jnp.float32)
    value = v_proj.astype(jnp.float32)
    grad = out_grad.astype(jnp.float32)
    gated = (key * value).astype(BF16)
    back_in = (grad * query).astype(BF16)
    conv_out, conv_grad, filter_grad = convolve(filter_taps, gated, back_in, blocks, inner_size)
    conv_out = conv_out.astype(jnp.float32)
    conv_grad = conv_grad.astype(jnp.float32)
    mixed = (query * conv_out).astype(BF16)
    q_grad = (grad * conv_out).astype(BF16)
    k_grad = (conv_grad * value).astype(BF16)
    v_grad = (conv_grad * key).astype(BF16)
    return (mixed, q_grad, k_grad, v_grad, filter_grad)


def solution(mesh):
    blocks = mesh.shape["ctx"] * mesh.shape["ch"]
    inner_size = mesh.shape["ch"]
    spec = P(("ctx", "ch"), None)

    def run(*arrays):
        tokens, channels = arrays[0].shape
        if channels == 128 * blocks and tokens == 128 * blocks:
            body = functools.partial(fast_body, blocks, inner_size)
        else:
            body = general_body
        return jax.shard_map(
            body, mesh=mesh, in_specs=(spec,) * 5, out_specs=(spec,) * 5, check_vma=False
        )(*arrays)

    return run
```

profile of v0, /device:TPU:0, one launch (start us, length us, event | category | flops | bytes accessed | tf_op | source)
XLA Modules:
  0.0 158.4 jit_solution(2500973609606413066)
XLA Ops:
  0.6 0.0 copy-start.1
  0.6 0.0 copy-start.2
  0.7 2.9 %fusion.1.back_ref = bf16[128,4096]{1,0:T(8,128)(2,1)} fusion(bf16[128,4096]{1,0:T(8,128)(2,1)} %param.9, bf16[128,4096]{1,0:T(8,128)(2,1)} %param.13), kind=kLoop, calls=%fused_computation.7 | loop fusion | flops 2097152 | bytes 3145728 | tf_op jit(solution)/shard_map/convert_element_type | solution.py:479
  3.6 0.0 copy-done.1
  3.6 0.0 copy-done.2
  3.6 0.0 copy-start
  3.6 0.2 fusion.gated_ref
  3.8 1.0 copy-done
  4.8 0.0 copy-start.3
  4.8 0.0 copy-start.4
  4.8 149.5 %shard_map.128 = (bf16[128,4096]{1,0:T(8,128)(2,1)S(1)}, bf16[128,4096]{1,0:T(8,128)(2,1)S(1)}, bf16[128,4096]{1,0:T(8,128)(2,1)S(1)}) custom-call(bf16[128,4096]{1,0:T(8,128)(2,1)S(1)} %copy-done, bf16[128,4096]{1,0:T(8,128)(2,1)S(1)} %fusion.gated_ref, bf16[128,4096]{1,0:T(8,128)(2,1)} %fusion.1.back_ref, bf16[1024,512]{1,0:T(8,128)(2,1)} %constant.8.clone.outer_hbm, ...), custom_call_target="tpu_custom_call" | custom-call | flops 11274289152 | bytes 16777216 | tf_op jit(solution)/shard_map/pallas_call | solution.py:447
  154.3 0.0 copy-done.3
  154.3 0.0 copy-done.4
  154.3 3.1 %fusion.3 = (bf16[128,4096]{1,0:T(8,128)(2,1)}, bf16[128,4096]{1,0:T(8,128)(2,1)}, bf16[128,4096]{1,0:T(8,128)(2,1)}, bf16[128,4096]{1,0:T(8,128)(2,1)}) fusion(bf16[128,4096]{1,0:T(8,128)(2,1)S(1)} %get-tuple-element.8, bf16[128,4096]{1,0:T(8,128)(2,1)S(1)} %copy-done.4, bf16[128,4096]{1,0:T(8,128)(2,1)S(1)} %copy-done.3, ...), kind=kLoop, calls=%fused_computation.9 | loop fusion | flops 7340032 | bytes 10485760 | tf_op jit(solution)/shard_map/convert_element_type | solution.py:484
  157.4 1.0 copy.15
Async XLA Ops:
  0.6 2.9 %copy-start.1 = (bf16[128,4096]{1,0:T(8,128)(2,1)S(1)}, bf16[128,4096]{1,0:T(8,128)(2,1)}, u32[]{:S(2)}) copy-start(bf16[128,4096]{1,0:T(8,128)(2,1)} %param.11) | copy-start | bytes 3145732
  0.6 2.9 %copy-start.2 = (bf16[128,4096]{1,0:T(8,128)(2,1)S(1)}, bf16[128,4096]{1,0:T(8,128)(2,1)}, u32[]{:S(2)}) copy-start(bf16[128,4096]{1,0:T(8,128)(2,1)} %param.10) | copy-start | bytes 3145732
  3.6 1.2 copy-start
  4.8 149.5 %copy-start.3 = (bf16[128,4096]{1,0:T(8,128)(2,1)S(1)}, bf16[128,4096]{1,0:T(8,128)(2,1)}, u32[]{:S(2)}) copy-start(bf16[128,4096]{1,0:T(8,128)(2,1)} %param.9) | copy-start | bytes 3145732
  4.8 149.5 %copy-start.4 = (bf16[128,4096]{1,0:T(8,128)(2,1)S(1)}, bf16[128,4096]{1,0:T(8,128)(2,1)}, u32[]{:S(2)}) copy-start(bf16[128,4096]{1,0:T(8,128)(2,1)} %param.13) | copy-start | bytes 3145732
where the time goes:
time: 159 us; the launch traced here: 158 us
  Pallas kernels  149 us (94%)
  other arithmetic  6.28 us (4%)
  local copies, waits for them, and re-layouts  1.95 us (1%)
    pallas_call x1, Pallas kernels, convolve(): pl.pallas_call(functools.partial(conv_kernel, blocks, inner_size), out_sh...  149 us

commit v1 on v0

--- a/solution.py
+++ b/solution.py
@@ -220,8 +220,10 @@
     blocks,
     inner_size,
     taps_ref,
-    gated_ref,
-    back_ref,
+    key_ref,
+    value_ref,
+    query_ref,
+    grad_ref,
     outer_hbm,
     inner_hbm,
     inner_inv_hbm,
@@ -235,18 +237,27 @@
     prod,
     taps_spec,
     gated_spec,
+    back_spec,
+    key_v,
+    value_v,
+    query_v,
+    grad_v,
+    gated_v,
+    back_v,
     outer_t,
     inner_t,
     inner_inv_t,
     outer_inv_t,
     table_sem,
+    load_sem,
     send_sem,
     recv_sem,
 ):
     rows = taps_ref.shape[0]
     lanes = rx.shape[-1]
     me = lax.axis_index("ctx") * inner_size + lax.axis_index("ch")
-    sources = (taps_ref, gated_ref, back_ref)
+    sources = (taps_ref, gated_v, back_v)
+    loads = ((key_ref, key_v), (value_ref, value_v), (query_ref, query_v), (grad_ref, grad_v))
     results = (conv_ref, cgrad_ref, fgrad_ref)
     tables = (
         (outer_hbm, outer_t),
@@ -310,9 +321,6 @@
         part = rx.at[0, pl.ds(0, (blocks - 1) * rows)]
         pltpu.make_async_copy(part, part, send_sem.at[slot]).wait()
 
-    for index, (source, target) in enumerate(tables):
-        pltpu.make_async_copy(source, target, table_sem.at[index]).start()
-
     barrier = pltpu.get_barrier_semaphore()
 
     @pl.loop(1, blocks)
@@ -320,11 +328,31 @@
         _, where = peer_at(step)
         pl.semaphore_signal(barrier, inc=1, device_id=where, device_id_type=MESH_ID)
 
+    for index, (source, target) in enumerate(loads):
+        pltpu.make_async_copy(source, target, load_sem.at[index]).start()
+
     pl.semaphore_wait(barrier, blocks - 1)
 
-    for which in range(3):
-        send_in(which)
-
+    send_in(0)
+
+    def gate(first, second, target):
+        for index in (first, second):
+            pltpu.make_async_copy(*loads[index], load_sem.at[index]).wait()
+
+        @pl.loop(0, rows // GROUP)
+        def _(group):
+            part = pl.ds(pl.multiple_of(group * GROUP, GROUP), GROUP)
+            left = loads[first][1][part, :].astype(jnp.float32)
+            right = loads[second][1][part, :].astype(jnp.float32)
+            target[part, :] = (left * right).astype(BF16)
+
+    gate(0, 1, gated_v)
+    send_in(1)
+    gate(2, 3, back_v)
+    send_in(2)
+
+    for index, (source, target) in enumerate(tables):
+        pltpu.make_async_copy(source, target, table_sem.at[index]).start()
     for index, (source, target) in enumerate(tables):
         pltpu.make_async_copy(source, target, table_sem.at[index]).wait()
 
@@ -372,7 +400,7 @@
             [jnp.where(alone, real, real + cross), jnp.where(alone, cross, li * rr - lr * ri)], axis=0
         ).astype(BF16)
 
-    def inverse_outer(which, slot):
+    def inverse_outer(which):
         signal = tx.at[which].reshape(blocks, rows, lanes)
 
         @pl.loop(0, pairs)
@@ -381,8 +409,8 @@
             high = pl.ds(pl.multiple_of(pair * 2 * GROUP + GROUP, GROUP), GROUP)
             data = jnp.concatenate(
                 [
-                    prod[slot, :, low, :].reshape(2 * blocks * GROUP, lanes),
-                    prod[slot, :, high, :].reshape(2 * blocks * GROUP, lanes),
+                    prod[:, low, :].reshape(2 * blocks * GROUP, lanes),
+                    prod[:, high, :].reshape(2 * blocks * GROUP, lanes),
                 ],
                 axis=1,
             )
@@ -390,44 +418,46 @@
             signal[:, low, :] = out[:, :lanes].reshape(blocks, GROUP, lanes)
             signal[:, high, :] = out[:, lanes:].reshape(blocks, GROUP, lanes)
 
+    def invert(k, pair):
+        out = jnp.dot(inner_inv_t[k], pair, preferred_element_type=jnp.float32)
+        prod[pl.ds(2 * k, 2)] = out.astype(BF16).reshape(2, rows, lanes)
+
     wait_in(0)
     outer_stage(0)
 
-    @pl.loop(0, blocks)
+    @pl.loop(0, blocks, unroll=2)
     def _(k):
         taps_spec[k] = spectrum(k)
 
     wait_in(1)
     outer_stage(1)
 
-    @pl.loop(0, blocks)
+    @pl.loop(0, blocks, unroll=2)
     def _(k):
         spec = spectrum(k)
         gated_spec[k] = spec
-        pair = multiply(taps_spec[k], spec, real_row(k))
-        out = jnp.dot(inner_inv_t[k], pair, preferred_element_type=jnp.float32)
-        prod[0, pl.ds(2 * k, 2)] = out.astype(BF16).reshape(2, rows, lanes)
-
-    inverse_outer(0, 0)
+        invert(k, multiply(taps_spec[k], spec, real_row(k)))
+
+    inverse_outer(0)
     send_out(0)
 
     wait_in(2)
     outer_stage(2)
 
-    @pl.loop(0, blocks)
+    @pl.loop(0, blocks, unroll=2)
     def _(k):
         spec = spectrum(k)
-        alone = real_row(k)
-        pair = jnp.concatenate(
-            [multiply_conj(spec, taps_spec[k], alone), multiply_conj(spec, gated_spec[k], alone)], axis=1
-        )
-        out = jnp.dot(inner_inv_t[k], pair, preferred_element_type=jnp.float32).astype(BF16)
-        prod[0, pl.ds(2 * k, 2)] = out[:, :lanes].reshape(2, rows, lanes)
-        prod[1, pl.ds(2 * k, 2)] = out[:, lanes:].reshape(2, rows, lanes)
-
-    inverse_outer(1, 0)
+        back_spec[k] = spec
+        invert(k, multiply_conj(spec, taps_spec[k], real_row(k)))
+
+    inverse_outer(1)
     send_out(1)
-    inverse_outer(2, 1)
+
+    @pl.loop(0, blocks, unroll=2)
+    def _(k):
+        invert(k, multiply_conj(back_spec[k], gated_spec[k], real_row(k)))
+
+    inverse_outer(2)
     send_out(2)
 
     for slot in range(6):
@@ -436,7 +466,7 @@
         wait_out(which)
 
 
-def convolve(taps, gated, back_in, blocks, inner_size):
+def convolve(taps, key, value, query, grad, blocks, inner_size):
     rows, channels = taps.shape
     lanes = channels // blocks
     norm_scale = 1.0 / math.sqrt(rows * blocks)
@@ -447,18 +477,21 @@
     return pl.pallas_call(
         functools.partial(conv_kernel, blocks, inner_size),
         out_shape=(signal, signal, signal),
-        in_specs=[anywhere] * 7,
+        in_specs=[pl.BlockSpec(memory_space=pltpu.HBM)] * 9,
         out_specs=(anywhere, anywhere, anywhere),
         scratch_shapes=[
             pltpu.VMEM((3, blocks * rows, lanes), BF16),
             pltpu.VMEM((3, blocks * rows, lanes), BF16),
             pltpu.VMEM((2 * blocks, rows, lanes), BF16),
-            pltpu.VMEM((2, 2 * blocks, rows, lanes), BF16),
+            pltpu.VMEM((2 * blocks, rows, lanes), BF16),
+            pltpu.VMEM((blocks, 2 * rows, lanes), jnp.float32),
             pltpu.VMEM((blocks, 2 * rows, lanes), jnp.float32),
             pltpu.VMEM((blocks, 2 * rows, lanes), jnp.float32),
         ]
+        + [pltpu.VMEM((rows, channels), BF16)] * 6
         + [pltpu.VMEM(table.shape, BF16) for table in tables]
         + [
+            pltpu.SemaphoreType.DMA((4,)),
             pltpu.SemaphoreType.DMA((4,)),
             pltpu.SemaphoreType.DMA((6,)),
             pltpu.SemaphoreType.DMA((6,)),
@@ -467,7 +500,7 @@
             collective_id=0, has_side_effects=True, vmem_limit_bytes=48 * 1024 * 1024
         ),
         cost_estimate=pl.CostEstimate(flops=flops, bytes_accessed=32 * rows * channels, transcendentals=0),
-    )(taps, gated, back_in, *(jnp.asarray(table) for table in tables))
+    )(taps, key, value, query, grad, *(jnp.asarray(table) for table in tables))
 
 
 def fast_body(blocks, inner_size, q_proj, k_proj, v_proj, filter_taps, out_grad):
@@ -475,9 +508,9 @@
     key = k_proj.astype(jnp.float32)
     value = v_proj.astype(jnp.float32)
     grad = out_grad.astype(jnp.float32)
-    gated = (key * value).astype(BF16)
-    back_in = (grad * query).astype(BF16)
-    conv_out, conv_grad, filter_grad = convolve(filter_taps, gated, back_in, blocks, inner_size)
+    conv_out, conv_grad, filter_grad = convolve(
+        filter_taps, k_proj, v_proj, q_proj, out_grad, blocks, inner_size
+    )
     conv_out = conv_out.astype(jnp.float32)
     conv_grad = conv_grad.astype(jnp.float32)
     mixed = (query * conv_out).astype(BF16)

time: 159 us -> 152 us (0.956)
  Pallas kernels: 149 us -> 144 us
  other arithmetic: 6.28 us -> 3.12 us
    pallas_call x1, Pallas kernels: 149 us -> 144 us  [convolve(): pl.pallas_call(functools.partial(conv_kernel, blocks, inner_size), out_sh...]
    convert_element_type x2 -> x0, other arithmetic: 3.16 us -> none  [the longest x1 2.91 us: fast_body(): back_in = (grad * query).astype(BF16)]
where the time goes in v1:
time: 152 us
  Pallas kernels  144 us (95%)
  local copies, waits for them, and re-layouts  3.42 us (2%)
  other arithmetic  3.12 us (2%)
    pallas_call x1, Pallas kernels, convolve(): pl.pallas_call(functools.partial(conv_kernel, blocks, inner_size), out_sh...  144 us
    unnamed x11, local copies, waits for them, and re-layouts  3.42 us
    convert_element_type x1, other arithmetic, fast_body(): q_grad = (grad * conv_out).astype(BF16)  3.12 us

profile of v1, /device:TPU:0, one launch (start us, length us, event | category | flops | bytes accessed | tf_op | source)
XLA Modules:
  0.0 151.6 jit_solution(4127537246277406531)
XLA Ops:
  0.6 0.0 copy-start
  0.6 1.2 copy-done
  1.9 0.0 copy-start.1
  1.9 1.2 copy-done.1
  3.1 0.0 copy-start.2
  3.1 0.0 copy-start.3
  3.1 0.0 copy-start.4
  3.1 144.4 %shard_map.128 = (bf16[128,4096]{1,0:T(8,128)(2,1)S(1)}, bf16[128,4096]{1,0:T(8,128)(2,1)S(1)}, bf16[128,4096]{1,0:T(8,128)(2,1)S(1)}) custom-call(bf16[128,4096]{1,0:T(8,128)(2,1)S(1)} %copy-done.1, bf16[128,4096]{1,0:T(8,128)(2,1)S(1)} %copy-done, bf16[128,4096]{1,0:T(8,128)(2,1)} %value_ref.1, bf16[128,4096]{1,0:T(8,128)(2,1)} %query_ref.1, ...), custom_call_target="tpu_custom_call" | custom-call | flops 11274289152 | bytes 16777216 | tf_op jit(solution)/shard_map/pallas_call | solution.py:477
  147.5 0.0 copy-done.2
  147.5 0.0 copy-done.3
  147.5 0.0 copy-done.4
  147.5 3.1 %fusion.1 = (bf16[128,4096]{1,0:T(8,128)(2,1)}, bf16[128,4096]{1,0:T(8,128)(2,1)}, bf16[128,4096]{1,0:T(8,128)(2,1)}, bf16[128,4096]{1,0:T(8,128)(2,1)}) fusion(bf16[128,4096]{1,0:T(8,128)(2,1)S(1)} %get-tuple-element.8, bf16[128,4096]{1,0:T(8,128)(2,1)S(1)} %copy-done.4, bf16[128,4096]{1,0:T(8,128)(2,1)S(1)} %copy-done.3, ...), kind=kLoop, calls=%fused_computation.5 | loop fusion | flops 7340032 | bytes 10485760 | tf_op jit(solution)/shard_map/convert_element_type | solution.py:517
  150.6 1.0 copy.15
Async XLA Ops:
  0.6 1.2 copy-start
  1.9 1.2 copy-start.1
  3.1 144.4 %copy-start.2 = (bf16[128,4096]{1,0:T(8,128)(2,1)S(1)}, bf16[128,4096]{1,0:T(8,128)(2,1)}, u32[]{:S(2)}) copy-start(bf16[128,4096]{1,0:T(8,128)(2,1)} %value_ref.1) | copy-start | bytes 3145732
  3.1 144.4 %copy-start.3 = (bf16[128,4096]{1,0:T(8,128)(2,1)S(1)}, bf16[128,4096]{1,0:T(8,128)(2,1)}, u32[]{:S(2)}) copy-start(bf16[128,4096]{1,0:T(8,128)(2,1)} %query_ref.1) | copy-start | bytes 3145732
  3.1 144.4 %copy-start.4 = (bf16[128,4096]{1,0:T(8,128)(2,1)S(1)}, bf16[128,4096]{1,0:T(8,128)(2,1)}, u32[]{:S(2)}) copy-start(bf16[128,4096]{1,0:T(8,128)(2,1)} %grad_ref.1) | copy-start | bytes 3145732

commit v2 on v1

--- a/solution.py
+++ b/solution.py
@@ -177,6 +177,7 @@
 
 MESH_ID = pl.DeviceIdType.MESH
 GROUP = 16
+VMEM_MIB = 57
 BF16 = jnp.bfloat16
 
 
@@ -228,8 +229,10 @@
     inner_hbm,
     inner_inv_hbm,
     outer_inv_hbm,
-    conv_ref,
-    cgrad_ref,
+    mixed_ref,
+    qgrad_ref,
+    kgrad_ref,
+    vgrad_ref,
     fgrad_ref,
     rx,
     tx,
@@ -244,12 +247,15 @@
     grad_v,
     gated_v,
     back_v,
+    conv_v,
+    cgrad_v,
     outer_t,
     inner_t,
     inner_inv_t,
     outer_inv_t,
     table_sem,
     load_sem,
+    store_sem,
     send_sem,
     recv_sem,
 ):
@@ -258,7 +264,7 @@
     me = lax.axis_index("ctx") * inner_size + lax.axis_index("ch")
     sources = (taps_ref, gated_v, back_v)
     loads = ((key_ref, key_v), (value_ref, value_v), (query_ref, query_v), (grad_ref, grad_v))
-    results = (conv_ref, cgrad_ref, fgrad_ref)
+    results = (conv_v, cgrad_v, fgrad_ref)
     tables = (
         (outer_hbm, outer_t),
         (inner_hbm, inner_t),
@@ -460,10 +466,65 @@
     inverse_outer(2)
     send_out(2)
 
+    def products(which, first, second):
+        wait_out(which)
+        source = results[which]
+
+        @pl.loop(0, rows // GROUP)
+        def _(group):
+            part = pl.ds(pl.multiple_of(group * GROUP, GROUP), GROUP)
+            conv = source[part, :].astype(jnp.float32)
+            for buffer, _, _ in (first, second):
+                buffer[part, :] = (buffer[part, :].astype(jnp.float32) * conv).astype(BF16)
+
+        for buffer, target, index in (first, second):
+            pltpu.make_async_copy(buffer, target, store_sem.at[index]).start()
+
+    stores = (
+        (query_v, mixed_ref, 0),
+        (grad_v, qgrad_ref, 1),
+        (value_v, kgrad_ref, 2),
+        (key_v, vgrad_ref, 3),
+    )
+    products(0, stores[0], stores[1])
+    products(1, stores[2], stores[3])
+
     for slot in range(6):
         wait_sent(slot)
-    for which in range(3):
-        wait_out(which)
+    for buffer, target, index in stores:
+        pltpu.make_async_copy(buffer, target, store_sem.at[index]).wait()
+    wait_out(2)
+
+
+def place_kernel(parts, *refs):
+    count = len(refs) // 2
+    sources, targets, sem = refs[:count], refs[count:-1], refs[-1]
+    size = sources[0].shape[0] // parts
+    copies = [
+        pltpu.make_async_copy(
+            sources[which].at[pl.ds(part * size, size)],
+            targets[which].at[pl.ds(part * size, size)],
+            sem.at[which * parts + part],
+        )
+        for part in range(parts)
+        for which in range(count)
+    ]
+    for copy in copies:
+        copy.start()
+    for copy in copies:
+        copy.wait()
+
+
+def place(results):
+    anywhere = pl.BlockSpec(memory_space=pl.ANY)
+    count, parts = len(results), 4
+    return pl.pallas_call(
+        functools.partial(place_kernel, parts),
+        out_shape=tuple(jax.ShapeDtypeStruct(result.shape, result.dtype) for result in results),
+        in_specs=[anywhere] * count,
+        out_specs=(anywhere,) * count,
+        scratch_shapes=[pltpu.SemaphoreType.DMA((count * parts,))],
+    )(*results)
 
 
 def convolve(taps, key, value, query, grad, blocks, inner_size):
@@ -476,9 +537,9 @@
     flops = 2 * lanes * 2 * rows * blocks * (9 * 2 * rows + 6 * blocks * GROUP)
     return pl.pallas_call(
         functools.partial(conv_kernel, blocks, inner_size),
-        out_shape=(signal, signal, signal),
+        out_shape=(signal,) * 5,
         in_specs=[pl.BlockSpec(memory_space=pltpu.HBM)] * 9,
-        out_specs=(anywhere, anywhere, anywhere),
+        out_specs=(anywhere,) * 5,
         scratch_shapes=[
             pltpu.VMEM((3, blocks * rows, lanes), BF16),
             pltpu.VMEM((3, blocks * rows, lanes), BF16),
@@ -488,36 +549,24 @@
             pltpu.VMEM((blocks, 2 * rows, lanes), jnp.float32),
             pltpu.VMEM((blocks, 2 * rows, lanes), jnp.float32),
         ]
-        + [pltpu.VMEM((rows, channels), BF16)] * 6
+        + [pltpu.VMEM((rows, channels), BF16)] * 8
         + [pltpu.VMEM(table.shape, BF16) for table in tables]
         + [
+            pltpu.SemaphoreType.DMA((4,)),
             pltpu.SemaphoreType.DMA((4,)),
             pltpu.SemaphoreType.DMA((4,)),
             pltpu.SemaphoreType.DMA((6,)),
             pltpu.SemaphoreType.DMA((6,)),
         ],
         compiler_params=pltpu.CompilerParams(
-            collective_id=0, has_side_effects=True, vmem_limit_bytes=48 * 1024 * 1024
+            collective_id=0, has_side_effects=True, vmem_limit_bytes=VMEM_MIB * 1024 * 1024
         ),
         cost_estimate=pl.CostEstimate(flops=flops, bytes_accessed=32 * rows * channels, transcendentals=0),
     )(taps, key, value, query, grad, *(jnp.asarray(table) for table in tables))
 
 
 def fast_body(blocks, inner_size, q_proj, k_proj, v_proj, filter_taps, out_grad):
-    query = q_proj.astype(jnp.float32)
-    key = k_proj.astype(jnp.float32)
-    value = v_proj.astype(jnp.float32)
-    grad = out_grad.astype(jnp.float32)
-    conv_out, conv_grad, filter_grad = convolve(
-        filter_taps, k_proj, v_proj, q_proj, out_grad, blocks, inner_size
-    )
-    conv_out = conv_out.astype(jnp.float32)
-    conv_grad = conv_grad.astype(jnp.float32)
-    mixed = (query * conv_out).astype(BF16)
-    q_grad = (grad * conv_out).astype(BF16)
-    k_grad = (conv_grad * value).astype(BF16)
-    v_grad = (conv_grad * key).astype(BF16)
-    return (mixed, q_grad, k_grad, v_grad, filter_grad)
+    return place(convolve(filter_taps, k_proj, v_proj, q_proj, out_grad, blocks, inner_size))
 
 
 def solution(mesh):

time: 152 us -> 306 us (2.01)
  Pallas kernels: 144 us -> 305 us
  local copies, waits for them, and re-layouts: 3.42 us -> 0 us
  other arithmetic: 3.12 us -> 0 us
    pallas_call x0 -> x1, Pallas kernels: none -> 160 us  [place(): pl.pallas_call(functools.partial(place_kernel, parts), out_shape=tuple((j...]
    unnamed x11 -> x0, local copies, waits for them, and re-layouts: 3.42 us -> none
    convert_element_type x1 -> x0, other arithmetic: 3.12 us -> none  [fast_body(): q_grad = (grad * conv_out).astype(BF16)]
where the time goes in v2:
time: 306 us
  Pallas kernels  305 us (100%)
    pallas_call x1, Pallas kernels, place(): pl.pallas_call(functools.partial(place_kernel, parts), out_shape=tuple((j...  160 us
    pallas_call x1, Pallas kernels, convolve(): pl.pallas_call(functools.partial(conv_kernel, blocks, inner_size), out_sh...  145 us

profile of v2, /device:TPU:0, one launch (start us, length us, event | category | flops | bytes accessed | tf_op | source)
XLA Modules:
  0.0 305.6 jit_solution(12526475501766955653)
XLA Ops:
  0.6 144.8 %shard_map.128 = (bf16[128,4096]{1,0:T(8,128)(2,1)}, bf16[128,4096]{1,0:T(8,128)(2,1)}, bf16[128,4096]{1,0:T(8,128)(2,1)}, bf16[128,4096]{1,0:T(8,128)(2,1)}, bf16[128,4096]{1,0:T(8,128)(2,1)}) custom-call(bf16[128,4096]{1,0:T(8,128)(2,1)} %taps_ref.1, bf16[128,4096]{1,0:T(8,128)(2,1)} %key_ref.1, bf16[128,4096]{1,0:T(8,128)(2,1)} %value_ref.1, ...), custom_call_target="tpu_custom_call" | custom-call | flops 11274289152 | bytes 16777216 | tf_op jit(solution)/shard_map/pallas_call | solution.py:538
  145.5 160.1 %shard_map.129 = (bf16[128,4096]{1,0:T(8,128)(2,1)}, bf16[128,4096]{1,0:T(8,128)(2,1)}, bf16[128,4096]{1,0:T(8,128)(2,1)}, bf16[128,4096]{1,0:T(8,128)(2,1)}, bf16[128,4096]{1,0:T(8,128)(2,1)}) custom-call(bf16[128,4096]{1,0:T(8,128)(2,1)} %get-tuple-element.10.refs_0_, bf16[128,4096]{1,0:T(8,128)(2,1)} %get-tuple-element.11.refs_1_, ...), custom_call_target="tpu_custom_call" | custom-call | tf_op jit(solution)/shard_map/pallas_call | solution.py:521

commit v3 on v2

--- a/solution.py
+++ b/solution.py
@@ -497,33 +497,42 @@
 
 
 def place_kernel(parts, *refs):
-    count = len(refs) // 2
-    sources, targets, sem = refs[:count], refs[count:-1], refs[-1]
+    count = (len(refs) - 3) // 2
+    sources, targets = refs[:count], refs[count : 2 * count]
+    staged, load_sem, store_sem = refs[2 * count :]
     size = sources[0].shape[0] // parts
-    copies = [
-        pltpu.make_async_copy(
-            sources[which].at[pl.ds(part * size, size)],
-            targets[which].at[pl.ds(part * size, size)],
-            sem.at[which * parts + part],
-        )
-        for part in range(parts)
-        for which in range(count)
-    ]
-    for copy in copies:
-        copy.start()
-    for copy in copies:
-        copy.wait()
+    loads, stores = [], []
+    for which in range(count):
+        for part in range(parts):
+            chunk = pl.ds(part * size, size)
+            index = which * parts + part
+            here = staged.at[which, chunk]
+            loads.append(pltpu.make_async_copy(sources[which].at[chunk], here, load_sem.at[index]))
+            stores.append(pltpu.make_async_copy(here, targets[which].at[chunk], store_sem.at[index]))
+    for load in loads:
+        load.start()
+    for load, store in zip(loads, stores):
+        load.wait()
+        store.start()
+    for store in stores:
+        store.wait()
 
 
 def place(results):
     anywhere = pl.BlockSpec(memory_space=pl.ANY)
     count, parts = len(results), 4
+    rows, channels = results[0].shape
     return pl.pallas_call(
         functools.partial(place_kernel, parts),
         out_shape=tuple(jax.ShapeDtypeStruct(result.shape, result.dtype) for result in results),
         in_specs=[anywhere] * count,
         out_specs=(anywhere,) * count,
-        scratch_shapes=[pltpu.SemaphoreType.DMA((count * parts,))],
+        scratch_shapes=[
+            pltpu.VMEM((count, rows, channels), BF16),
+            pltpu.SemaphoreType.DMA((count * parts,)),
+            pltpu.SemaphoreType.DMA((count * parts,)),
+        ],
+        compiler_params=pltpu.CompilerParams(vmem_limit_bytes=VMEM_MIB * 1024 * 1024),
     )(*results)
 
 

time: 306 us -> 151 us (0.49)
  Pallas kernels: 305 us -> 150 us
    pallas_call x1, Pallas kernels: 160 us -> 5.01 us  [place(): pl.pallas_call(functools.partial(place_kernel, parts), out_shape=tuple((j...]
where the time goes in v3:
time: 151 us; the launch traced here: 150 us
  Pallas kernels  150 us (99%)
    pallas_call x1, Pallas kernels, convolve(): pl.pallas_call(functools.partial(conv_kernel, blocks, inner_size), out_sh...  145 us
    pallas_call x1, Pallas kernels, place(): pl.pallas_call(functools.partial(place_kernel, parts), out_shape=tuple((j...  5.01 us

profile of v3, /device:TPU:0, one launch (start us, length us, event | category | flops | bytes accessed | tf_op | source)
XLA Modules:
  0.0 150.5 jit_solution(1748678944548966324)
XLA Ops:
  0.6 144.8 %shard_map.128 = (bf16[128,4096]{1,0:T(8,128)(2,1)}, bf16[128,4096]{1,0:T(8,128)(2,1)}, bf16[128,4096]{1,0:T(8,128)(2,1)}, bf16[128,4096]{1,0:T(8,128)(2,1)}, bf16[128,4096]{1,0:T(8,128)(2,1)}) custom-call(bf16[128,4096]{1,0:T(8,128)(2,1)} %taps_ref.1, bf16[128,4096]{1,0:T(8,128)(2,1)} %key_ref.1, bf16[128,4096]{1,0:T(8,128)(2,1)} %value_ref.1, ...), custom_call_target="tpu_custom_call" | custom-call | flops 11274289152 | bytes 16777216 | tf_op jit(solution)/shard_map/pallas_call | solution.py:547
  145.5 5.0 %shard_map.129 = (bf16[128,4096]{1,0:T(8,128)(2,1)}, bf16[128,4096]{1,0:T(8,128)(2,1)}, bf16[128,4096]{1,0:T(8,128)(2,1)}, bf16[128,4096]{1,0:T(8,128)(2,1)}, bf16[128,4096]{1,0:T(8,128)(2,1)}) custom-call(bf16[128,4096]{1,0:T(8,128)(2,1)} %get-tuple-element.10.refs_0_, bf16[128,4096]{1,0:T(8,128)(2,1)} %get-tuple-element.11.refs_1_, ...), custom_call_target="tpu_custom_call" | custom-call | tf_op jit(solution)/shard_map/pallas_call | solution.py:525
